TPU v7x, 256 devices: a whole 4x4x8 slice. The times are simulated.
256 devices in a mesh: tm: 16 (over z, core), row: 16 (over x, y).
Axes of the slice: x: 4, y: 4, z: 8, core: 2. Of those that a mesh axis runs over, the one named last changes fastest.
Arguments:
- hidden_state: bfloat16 [2, 48, 16, 160, 512], P(None, 'tm', 'row'), may hold values from -64 to 64
- grad_out: bfloat16 [2, 48, 16, 160, 512], P(None, 'tm', 'row'), may hold values from -6 to 6
- norm_gain: float32 [512], replicated, may hold values from 0.1 to 1.9
- norm_shift: float32 [512], replicated, may hold values from -4 to 4
- conv_weight: bfloat16 [512, 27, 512], P('row'), may hold values from -0.0546875 to 0.0546875
Outputs:
- grad_hidden: bfloat16 [2, 48, 16, 160, 512], P(None, 'tm', 'row')
All inputs are finite; a program needn't handle non-finite values.
Results may differ from a plain program's by a relative error of at most 0.001.
Values may be sent and summed in bfloat16 or wider, within the bound.
A program may use at most 192 MiB of HBM per device.

v0:
```python
import jax
import jax.numpy as jnp
from jax import lax
from jax.sharding import PartitionSpec as P

GROUPS = 32


def passed_along(value, axis, steps):
    count = lax.axis_size(axis)
    leading, last = (max(0, -steps), min(count, count - steps))
    return lax.ppermute(value, axis, [(source, source + steps) for source in range(leading, last)])


def padded_2(block, sides, width):
    for axis, dim in sides:
        count = lax.axis_size(axis)
        forward = [(i, i + 1) for i in range(count - 1)]
        backward = [(target, source) for source, target in forward]
        low = lax.ppermute(
            lax.slice_in_dim(block, block.shape[dim] - width, None, axis=dim), axis, forward
        )
        high = lax.ppermute(lax.slice_in_dim(block, 0, width, axis=dim), axis, backward)
        block = jnp.concatenate([low, block, high], axis=dim)
    return block


def shards(hidden_state, grad_out, norm_gain, norm_shift, conv_weight):
    hidden_f = hidden_state.astype(jnp.float32)
    clips, frames, rows, width, chan = hidden_f.shape
    per = chan // GROUPS
    count = frames * lax.axis_size("tm") * rows * lax.axis_size("row") * width * per

    def group_sum(value):
        return jnp.sum(value, axis=(1, 2, 3)).reshape(clips, GROUPS, per).sum(-1)

    def spread(stat):
        return jnp.repeat(stat, per, axis=1)[:, None, None, None, :]

    mean = lax.psum(group_sum(hidden_f), ("tm", "row")) / count
    centered = hidden_f - spread(mean)
    variance = lax.psum(group_sum(centered * centered), ("tm", "row")) / count
    rstd = lax.rsqrt(variance + 1e-06)
    normed = centered * spread(rstd)
    pre = normed * norm_gain + norm_shift
    following = passed_along(grad_out[:, :2], "tm", -1)
    extended = jnp.concatenate([grad_out, following], axis=1)
    rimmed = padded_2(extended, (("row", 2),), 1)
    padded = jnp.pad(rimmed, ((0, 0), (0, 0), (0, 0), (1, 1), (0, 0)))
    full_kernel = lax.all_gather(conv_weight, "row", axis=0, tiled=True)
    total = jnp.zeros((clips, frames, rows, width, full_kernel.shape[0]), jnp.float32)
    for kt in range(3):
        for kr in range(3):
            for kw in range(3):
                window = padded[
                    :, 2 - kt : 2 - kt + frames, 2 - kr : 2 - kr + rows, 2 - kw : 2 - kw + width, :
                ]
                total = total + jnp.einsum(
                    "bfrwo,io->bfrwi",
                    window,
                    full_kernel[:, 9 * kt + 3 * kr + kw, :],
                    preferred_element_type=jnp.float32,
                )
    sig = jax.nn.sigmoid(pre)
    slope = sig * (1.0 + pre * (1.0 - sig))
    grad_pre = total * slope * norm_gain
    first_sum, second_sum = lax.psum(
        (group_sum(grad_pre), group_sum(grad_pre * normed)), ("tm", "row")
    )
    first = first_sum / count
    second = second_sum / count
    grad_hidden = spread(rstd) * (grad_pre - spread(first) - normed * spread(second))
    return grad_hidden.astype(jnp.bfloat16)


def solution(mesh):
    return jax.shard_map(
        shards,
        mesh=mesh,
        in_specs=(
            P(None, "tm", "row", None, None),
            P(None, "tm", "row", None, None),
            P(),
            P(),
            P("row", None, None),
        ),
        out_specs=P(None, "tm", "row", None, None),
        check_vma=False,
    )
```

profile of v0, /device:TPU:1, one launch (start us, length us, event | category | flops | bytes accessed | tf_op | source)
XLA Modules:
  0.0 390.0 jit_solution(3871283386164522698)
XLA Ops:
  6.5 0.7 all-gather.2.cloned.1.call-update
  7.3 1.1 slice.235
  8.4 5.3 %collective-permute-start = (bf16[2,2,1,160,512]{4,3,1,0,2:T(8,128)(2,1)S(1)}, bf16[2,2,1,160,512]{4,3,1,0,2:T(8,128)(2,1)S(1)}, u32[]{:S(2)}, u32[]{:S(2)}) collective-permute-start(bf16[2,2,1,160,512]{4,3,1,0,2:T(8,128)(2,1)S(1)} %slice.235), channel_id=1, source_target_pairs={{16,0},{32,16},{48,32},{64,48},{80,64},{96,80},{112,96},{128,112},... | collective-permute-start | bytes 1966088 | tf_op jit(solution)/shard_map/ppermute | solution.py:12
  13.7 8.0 %collective-permute-done = bf16[2,2,1,160,512]{4,3,1,0,2:T(8,128)(2,1)S(1)} collective-permute-done((bf16[2,2,1,160,512]{4,3,1,0,2:T(8,128)(2,1)S(1)}, bf16[2,2,1,160,512]{4,3,1,0,2:T(8,128)(2,1)S(1)}, u32[]{:S(2)}, u32[]{:S(2)}) %collective-permute-start) | collective-permute-done | bytes 655392 | tf_op jit(solution)/shard_map/ppermute | solution.py:12
  21.7 1.3 pad_maximum_fusion
  23.0 1.3 collective-permute-start.2
  24.3 5.5 %collective-permute-start.1 = (bf16[2,5,1,160,512]{4,3,1,0,2:T(8,128)(2,1)}, bf16[2,5,1,160,512]{4,3,1,0,2:T(8,128)(2,1)}, u32[]{:S(2)}, u32[]{:S(2)}) collective-permute-start(bf16[2,5,1,160,512]{4,3,1,0,2:T(8,128)(2,1)} %pad_maximum_fusion), channel_id=1, source_target_pairs={{0,1},{1,2},{2,3},{3,4},{4,5},{5,6},{6,7},{7,8},{8,9},{9,10},{10,1... | collective-permute-start | bytes 4915208 | tf_op jit(solution)/shard_map/ppermute | solution.py:20
  29.8 0.2 convert_reduce_fusion
  30.1 0.1 reduce_sum.73
  30.1 117.8 %psum.28 = f32[2,32]{1,0:T(2,128)S(1)} all-reduce(f32[2,32]{1,0:T(2,128)S(1)} %reduce_sum.73), channel_id=1, replica_groups=mesh['tm'=16,'row'=16] {'tm','row'}, use_global_device_ids=true, to_apply=%region_2.0 | all-reduce | flops 64 | bytes 512 | tf_op jit(solution)/shard_map/psum | solution.py:40
  148.0 0.1 sub.26
  148.1 0.3 fusion.23
  148.5 0.1 reduce_sum.75
  148.5 72.4 %psum.29 = f32[2,32]{1,0:T(2,128)S(1)} all-reduce(f32[2,32]{1,0:T(2,128)S(1)} %reduce_sum.75), channel_id=1, replica_groups=mesh['tm'=16,'row'=16] {'tm','row'}, use_global_device_ids=true, to_apply=%region_5.0 | all-reduce | flops 64 | bytes 512 | tf_op jit(solution)/shard_map/psum | solution.py:42
  221.0 0.1 mul.56
  221.2 6.8 %select_maximum_fusion = bf16[2,5,3,162,512]{4,3,1,0,2:T(8,128)(2,1)} fusion(bf16[2,5,1,160,512]{4,3,1,0,2:T(8,128)(2,1)} %collective-permute-done.2, bf16[2,5,1,160,512]{4,3,1,0,2:T(8,128)(2,1)} %collective-permute-done.1, bf16[2,2,1,160,512]{4,3,1,0,2:T(8,128)(2,1)S(1)} %collective-permute-done, bf16[2,3,1,160,512]{4,3,1,0,2:T(8,128)(2,1)S(1)} %bitcast.292), kind=kLoop, calls=%fused_computation.3 | loop fusion | flops 37324800 | bytes 9891840 | tf_op jit(solution)/shard_map/concatenate | solution.py:24
  227.9 3.5 fusion.34
  231.4 4.1 %fusion.42 = f32[2,3,160,512]{3,2,1,0:T(8,128)} fusion(bf16[2,5,1,160,512]{4,3,1,0,2:T(8,128)(2,1)} %collective-permute-done.1, bf16[512,27,512]{2,0,1:T(8,128)(2,1)} %all-gather.2.cloned.1.call-done), kind=kOutput, calls=%fused_computation.61 | convolution fusion | flops 503316480 | bytes 3473408 | tf_op jit(solution)/shard_map/bfrwo,io->bfrwi/dot_general | solution.py:58
  235.5 3.4 fusion.50
  238.9 3.5 fusion.39
  242.4 3.3 fusion.47
  245.7 3.2 fusion.55
  248.9 2.0 fusion.35
  250.9 2.0 fusion.36
  252.9 2.0 fusion.37
  254.9 2.0 fusion.38
  256.9 2.0 fusion.40
  258.9 2.0 fusion.41
  260.9 2.0 fusion.43
  263.0 2.0 fusion.44
  265.0 2.0 fusion.45
  267.0 2.1 fusion.46
  269.0 2.0 fusion.48
  271.0 2.0 fusion.49
  273.0 2.0 fusion.51
  275.0 1.9 fusion.52
  276.9 2.0 fusion.53
  278.9 2.0 fusion.54
  280.9 2.0 fusion.56
  282.9 2.2 fusion.26
  285.2 2.0 fusion.30
  287.2 2.0 fusion.57
  289.1 17.8 %fusion.61 = (f32[2,512]{1,0:T(2,128)S(1)}, f32[2,512]{1,0:T(2,128)S(1)}, f32[2,3,1,160,512]{4,3,1,0,2:T(8,128)S(1)}) fusion(f32[2,512]{1,0:T(2,128)S(1)} %mul.56, f32[2,512]{1,0:T(2,128)S(1)} %sub.26, bf16[2,3,1,160,512]{4,3,2,1,0:T(8,128)(2,1)S(1)} %copy-done, f32[512]{0:T(512)S(1)} %copy-done.3, f32[512]{0:T(512)S(1)} %copy-done.4, ...), kind=kOutput, calls=%fused_computation.125 | convolution fusion | flops 524449792 | bytes 55595008 | tf_op jit(solution)/shard_map/bfrwo,io->bfrwi/dot_general | solution.py:58
  307.2 0.1 reduce_sum.79
  307.3 74.1 %all-reduce.1 = (f32[2,32]{1,0:T(2,128)S(1)}, f32[2,32]{1,0:T(2,128)S(1)}) all-reduce(f32[2,32]{1,0:T(2,128)S(1)} %reduce_sum.79, f32[2,32]{1,0:T(2,128)S(1)} %reduce_sum.77), channel_id=1, replica_groups=mesh['tm'=16,'row'=16] {'tm','row'}, use_global_device_ids=true, to_apply=%region_11.12 | all-reduce | flops 128 | bytes 1024 | tf_op jit(solution)/shard_map/psum | solution.py:67
  381.5 0.1 mul.66
  381.7 0.1 sub.30
  381.8 1.4 fusion.32
  (31 shorter events, 0.8 us)
Async XLA Ops:
  6.5 15.2 %copy-start.1 = (bf16[2,3,1,160,512]{4,3,2,1,0:T(8,128)(2,1)S(1)}, bf16[2,3,1,160,512]{4,3,2,1,0:T(8,128)(2,1)}, u32[]{:S(2)}) copy-start(bf16[2,3,1,160,512]{4,3,2,1,0:T(8,128)(2,1)} %param.6) | copy-start | bytes 2949124
  6.5 221.4 %all-gather.2.cloned.1.call-start = ((), (), s32[]{:S(2)}) async-start(), calls=%async_computation | async-start | bytes 15040512 | tf_op jit(solution)/shard_map/all_gather | solution.py:50
  8.4 21.4 %copy-start = (bf16[2,3,1,160,512]{4,3,2,1,0:T(8,128)(2,1)S(1)}, bf16[2,3,1,160,512]{4,3,2,1,0:T(8,128)(2,1)}, u32[]{:S(2)}) copy-start(bf16[2,3,1,160,512]{4,3,2,1,0:T(8,128)(2,1)} %param.5) | copy-start | bytes 2949124
  8.4 13.3 %collective-permute-start = (bf16[2,2,1,160,512]{4,3,1,0,2:T(8,128)(2,1)S(1)}, bf16[2,2,1,160,512]{4,3,1,0,2:T(8,128)(2,1)S(1)}, u32[]{:S(2)}, u32[]{:S(2)}) collective-permute-start(bf16[2,2,1,160,512]{4,3,1,0,2:T(8,128)(2,1)S(1)} %slice.235), channel_id=1, source_target_pairs={{16,0},{32,16},{48,32},{64,48},{80,64},{96,80},{112,96},{128,112},... | collective-permute-start | bytes 1966088 | tf_op jit(solution)/shard_map/ppermute | solution.py:12
  23.0 198.1 %collective-permute-start.2 = (bf16[2,5,1,160,512]{4,3,1,0,2:T(8,128)(2,1)}, bf16[2,5,1,160,512]{4,3,1,0,2:T(8,128)(2,1)}, u32[]{:S(2)}, u32[]{:S(2)}) collective-permute-start(bf16[2,5,1,160,512]{4,3,1,0,2:T(8,128)(2,1)} %pad_maximum_fusion), channel_id=1, source_target_pairs={{1,0},{2,1},{3,2},{4,3},{5,4},{6,5},{7,6},{8,7},{9,8},{10,9},{11,1... | collective-permute-start | bytes 4915208 | tf_op jit(solution)/shard_map/ppermute | solution.py:23
  24.3 196.8 %collective-permute-start.1 = (bf16[2,5,1,160,512]{4,3,1,0,2:T(8,128)(2,1)}, bf16[2,5,1,160,512]{4,3,1,0,2:T(8,128)(2,1)}, u32[]{:S(2)}, u32[]{:S(2)}) collective-permute-start(bf16[2,5,1,160,512]{4,3,1,0,2:T(8,128)(2,1)} %pad_maximum_fusion), channel_id=1, source_target_pairs={{0,1},{1,2},{2,3},{3,4},{4,5},{5,6},{6,7},{7,8},{8,9},{9,10},{10,1... | collective-permute-start | bytes 4915208 | tf_op jit(solution)/shard_map/ppermute | solution.py:20
  227.9 17.7 %copy-start.2 = (bf16[512,27,512]{2,0,1:T(8,128)(2,1)S(1)}, bf16[512,27,512]{2,0,1:T(8,128)(2,1)}, u32[]{:S(2)}) copy-start(bf16[512,27,512]{2,0,1:T(8,128)(2,1)} %all-gather.2.cloned.1.call-done) | copy-start | bytes 42467332
  231.4 17.5 %slice-start = ((s8[5160960]{0:T(1024)(128)(4,1)}), s8[4194304]{0:T(1024)(128)(4,1)S(1)}, s32[]{:S(2)}) async-start(s8[5160960]{0:T(1024)(128)(4,1)} %bitcast.288), calls=%async_computation.1 | async-start | bytes 8388608
  238.9 10.0 %slice-start.1 = ((s8[5160960]{0:T(1024)(128)(4,1)}), s8[966656]{0:T(1024)(128)(4,1)S(1)}, s32[]{:S(2)}) async-start(s8[5160960]{0:T(1024)(128)(4,1)} %bitcast.288), calls=%async_computation.2 | async-start | bytes 1933312
  287.2 2.0 copy-start.3
  287.2 2.0 copy-start.4
Sparse Core Ops, SparseCore 0:
  9.8 141.7 all-gather.1
where the time goes:
time: 391 us; the launch traced here: 390 us
  blocking collectives  264 us (68%)
  matrix products  79 us (20%)
  between operations  13.5 us (3%)
  starting transfers between devices  12 us (3%)
  other arithmetic  10.3 us (3%)
  waiting for transfers between devices  8.76 us (2%)
    psum x1, blocking collectives, shards(): mean = lax.psum(group_sum(hidden_f), ('tm', 'row')) / count  118 us
    dot_general x27, matrix products, shards(): jnp.einsum('bfrwo,io->bfrwi', window, full_kernel[:, 9 * kt + 3 * kr + kw...  79 us
    psum x1, blocking collectives, shards(): lax.psum((group_sum(grad_pre), group_sum(grad_pre * normed)), ('tm', 'row'))  74.1 us
    psum x1, blocking collectives, shards(): variance = lax.psum(group_sum(centered * centered), ('tm', 'row')) / count  72.4 us
    ppermute x1, waiting for transfers between devices, passed_along(): lax.ppermute(value, axis, [(source, source + steps) for source in range(l...  8.04 us
  transfers between devices with their start and end apart: 4, of which 1 were waited for; matrix products, arithmetic and copies ran while one was open for 3% of the time, Pallas kernels for 0%

commit v1 on v0

--- a/solution.py
+++ b/solution.py
@@ -37,7 +37,7 @@
     def spread(stat):
         return jnp.repeat(stat, per, axis=1)[:, None, None, None, :]
 
-    mean = lax.psum(group_sum(hidden_f), ("tm", "row")) / count
+    mean = lax.psum(lax.psum(group_sum(hidden_f), "tm"), "row") / count
     centered = hidden_f - spread(mean)
     variance = lax.psum(group_sum(centered * centered), ("tm", "row")) / count
     rstd = lax.rsqrt(variance + 1e-06)

time: 391 us -> 356 us (0.910)
  blocking collectives: 264 us -> 229 us
    psum x1 -> x2, blocking collectives: 118 us -> 70 us  [shards(): mean = lax.psum(lax.psum(group_sum(hidden_f), 'tm'), 'row') / count]
    psum x1, blocking collectives: 72.4 us -> 84.7 us  [shards(): variance = lax.psum(group_sum(centered * centered), ('tm', 'row')) / count]
where the time goes in v1:
time: 356 us; the launch traced here: 355 us
  blocking collectives  229 us (64%)
  matrix products  79 us (22%)
  between operations  13.5 us (4%)
  starting transfers between devices  12 us (3%)
  other arithmetic  10.3 us (3%)
  waiting for transfers between devices  8.76 us (2%)
    psum x1, blocking collectives, shards(): variance = lax.psum(group_sum(centered * centered), ('tm', 'row')) / count  84.7 us
    dot_general x27, matrix products, shards(): jnp.einsum('bfrwo,io->bfrwi', window, full_kernel[:, 9 * kt + 3 * kr + kw...  79 us
    psum x1, blocking collectives, shards(): lax.psum((group_sum(grad_pre), group_sum(grad_pre * normed)), ('tm', 'row'))  74.7 us
    psum x2, blocking collectives, shards(): mean = lax.psum(lax.psum(group_sum(hidden_f), 'tm'), 'row') / count  70 us
    ppermute x1, waiting for transfers between devices, passed_along(): lax.ppermute(value, axis, [(source, source + steps) for source in range(l...  8.04 us
  transfers between devices with their start and end apart: 4, of which 1 were waited for; matrix products, arithmetic and copies ran while one was open for 3% of the time, Pallas kernels for 0%

profile of v1, /device:TPU:1, one launch (start us, length us, event | category | flops | bytes accessed | tf_op | source)
XLA Modules:
  0.0 355.3 jit_solution(499955819977418457)
XLA Ops:
  6.5 0.7 all-gather.2.cloned.1.call-update
  7.3 1.1 slice.235
  8.4 5.3 %collective-permute-start = (bf16[2,2,1,160,512]{4,3,1,0,2:T(8,128)(2,1)S(1)}, bf16[2,2,1,160,512]{4,3,1,0,2:T(8,128)(2,1)S(1)}, u32[]{:S(2)}, u32[]{:S(2)}) collective-permute-start(bf16[2,2,1,160,512]{4,3,1,0,2:T(8,128)(2,1)S(1)} %slice.235), channel_id=1, source_target_pairs={{16,0},{32,16},{48,32},{64,48},{80,64},{96,80},{112,96},{128,112},... | collective-permute-start | bytes 1966088 | tf_op jit(solution)/shard_map/ppermute | solution.py:12
  13.7 8.0 %collective-permute-done = bf16[2,2,1,160,512]{4,3,1,0,2:T(8,128)(2,1)S(1)} collective-permute-done((bf16[2,2,1,160,512]{4,3,1,0,2:T(8,128)(2,1)S(1)}, bf16[2,2,1,160,512]{4,3,1,0,2:T(8,128)(2,1)S(1)}, u32[]{:S(2)}, u32[]{:S(2)}) %collective-permute-start) | collective-permute-done | bytes 655392 | tf_op jit(solution)/shard_map/ppermute | solution.py:12
  21.7 1.3 pad_maximum_fusion
  23.0 1.3 collective-permute-start.2
  24.3 5.5 %collective-permute-start.1 = (bf16[2,5,1,160,512]{4,3,1,0,2:T(8,128)(2,1)}, bf16[2,5,1,160,512]{4,3,1,0,2:T(8,128)(2,1)}, u32[]{:S(2)}, u32[]{:S(2)}) collective-permute-start(bf16[2,5,1,160,512]{4,3,1,0,2:T(8,128)(2,1)} %pad_maximum_fusion), channel_id=1, source_target_pairs={{0,1},{1,2},{2,3},{3,4},{4,5},{5,6},{6,7},{7,8},{8,9},{9,10},{10,1... | collective-permute-start | bytes 4915208 | tf_op jit(solution)/shard_map/ppermute | solution.py:20
  29.8 0.2 convert_reduce_fusion
  30.1 25.6 %psum.35 = f32[2,32]{1,0:T(2,128)S(1)} all-reduce(f32[2,32]{1,0:T(2,128)S(1)} %reduce_sum.73), channel_id=1, replica_groups=mesh['tm'=16,'row'=16] {'tm'}, use_global_device_ids=true, to_apply=%region_2.0 | all-reduce | flops 64 | bytes 512 | tf_op jit(solution)/shard_map/psum | solution.py:40
  55.8 44.4 %psum.36 = f32[2,32]{1,0:T(2,128)S(1)} all-reduce(f32[2,32]{1,0:T(2,128)S(1)} %psum.35), channel_id=1, replica_groups=mesh['tm'=16,'row'=16] {'row'}, use_global_device_ids=true, to_apply=%region_3.0 | all-reduce | flops 64 | bytes 512 | tf_op jit(solution)/shard_map/psum | solution.py:40
  100.3 0.1 sub.26
  100.4 0.3 fusion.23
  100.7 0.1 reduce_sum.75
  100.8 84.7 %psum.37 = f32[2,32]{1,0:T(2,128)S(1)} all-reduce(f32[2,32]{1,0:T(2,128)S(1)} %reduce_sum.75), channel_id=1, replica_groups=mesh['tm'=16,'row'=16] {'tm','row'}, use_global_device_ids=true, to_apply=%region_6.0 | all-reduce | flops 64 | bytes 512 | tf_op jit(solution)/shard_map/psum | solution.py:42
  185.6 0.1 mul.56
  185.7 6.8 %select_maximum_fusion = bf16[2,5,3,162,512]{4,3,1,0,2:T(8,128)(2,1)} fusion(bf16[2,5,1,160,512]{4,3,1,0,2:T(8,128)(2,1)} %collective-permute-done.2, bf16[2,5,1,160,512]{4,3,1,0,2:T(8,128)(2,1)} %collective-permute-done.1, bf16[2,2,1,160,512]{4,3,1,0,2:T(8,128)(2,1)S(1)} %collective-permute-done, bf16[2,3,1,160,512]{4,3,1,0,2:T(8,128)(2,1)S(1)} %bitcast.292), kind=kLoop, calls=%fused_computation.3 | loop fusion | flops 37324800 | bytes 9891840 | tf_op jit(solution)/shard_map/concatenate | solution.py:24
  192.5 3.5 fusion.34
  196.0 4.1 %fusion.42 = f32[2,3,160,512]{3,2,1,0:T(8,128)} fusion(bf16[2,5,1,160,512]{4,3,1,0,2:T(8,128)(2,1)} %collective-permute-done.1, bf16[512,27,512]{2,0,1:T(8,128)(2,1)} %all-gather.2.cloned.1.call-done), kind=kOutput, calls=%fused_computation.61 | convolution fusion | flops 503316480 | bytes 3473408 | tf_op jit(solution)/shard_map/bfrwo,io->bfrwi/dot_general | solution.py:58
  200.1 3.4 fusion.50
  203.4 3.5 fusion.39
  206.9 3.3 fusion.47
  210.2 3.2 fusion.55
  213.4 2.0 fusion.35
  215.4 2.0 fusion.36
  217.4 2.0 fusion.37
  219.4 2.0 fusion.38
  221.4 2.0 fusion.40
  223.5 2.0 fusion.41
  225.5 2.0 fusion.43
  227.5 2.0 fusion.44
  229.5 2.0 fusion.45
  231.5 2.1 fusion.46
  233.6 2.0 fusion.48
  235.6 2.0 fusion.49
  237.5 2.0 fusion.51
  239.5 1.9 fusion.52
  241.5 2.0 fusion.53
  243.5 2.0 fusion.54
  245.5 2.0 fusion.56
  247.5 2.2 fusion.26
  249.7 2.0 fusion.30
  251.7 2.0 fusion.57
  253.7 17.8 %fusion.61 = (f32[2,512]{1,0:T(2,128)S(1)}, f32[2,512]{1,0:T(2,128)S(1)}, f32[2,3,1,160,512]{4,3,1,0,2:T(8,128)S(1)}) fusion(f32[2,512]{1,0:T(2,128)S(1)} %mul.56, f32[2,512]{1,0:T(2,128)S(1)} %sub.26, bf16[2,3,1,160,512]{4,3,2,1,0:T(8,128)(2,1)S(1)} %copy-done, f32[512]{0:T(512)S(1)} %copy-done.3, f32[512]{0:T(512)S(1)} %copy-done.4, ...), kind=kOutput, calls=%fused_computation.125 | convolution fusion | flops 524449792 | bytes 55595008 | tf_op jit(solution)/shard_map/bfrwo,io->bfrwi/dot_general | solution.py:58
  271.6 0.1 reduce_sum.77
  271.8 0.1 reduce_sum.79
  271.9 74.7 %all-reduce.1 = (f32[2,32]{1,0:T(2,128)S(1)}, f32[2,32]{1,0:T(2,128)S(1)}) all-reduce(f32[2,32]{1,0:T(2,128)S(1)} %reduce_sum.79, f32[2,32]{1,0:T(2,128)S(1)} %reduce_sum.77), channel_id=1, replica_groups=mesh['tm'=16,'row'=16] {'tm','row'}, use_global_device_ids=true, to_apply=%region_12.13 | all-reduce | flops 128 | bytes 1024 | tf_op jit(solution)/shard_map/psum | solution.py:67
  346.9 0.1 sub.30
  347.0 1.4 fusion.32
  (32 shorter events, 0.8 us)
Async XLA Ops:
  6.5 15.2 %copy-start.1 = (bf16[2,3,1,160,512]{4,3,2,1,0:T(8,128)(2,1)S(1)}, bf16[2,3,1,160,512]{4,3,2,1,0:T(8,128)(2,1)}, u32[]{:S(2)}) copy-start(bf16[2,3,1,160,512]{4,3,2,1,0:T(8,128)(2,1)} %param.6) | copy-start | bytes 2949124
  6.5 186.0 %all-gather.2.cloned.1.call-start = ((), (), s32[]{:S(2)}) async-start(), calls=%async_computation | async-start | bytes 15040512 | tf_op jit(solution)/shard_map/all_gather | solution.py:50
  8.4 21.4 %copy-start = (bf16[2,3,1,160,512]{4,3,2,1,0:T(8,128)(2,1)S(1)}, bf16[2,3,1,160,512]{4,3,2,1,0:T(8,128)(2,1)}, u32[]{:S(2)}) copy-start(bf16[2,3,1,160,512]{4,3,2,1,0:T(8,128)(2,1)} %param.5) | copy-start | bytes 2949124
  8.4 13.3 %collective-permute-start = (bf16[2,2,1,160,512]{4,3,1,0,2:T(8,128)(2,1)S(1)}, bf16[2,2,1,160,512]{4,3,1,0,2:T(8,128)(2,1)S(1)}, u32[]{:S(2)}, u32[]{:S(2)}) collective-permute-start(bf16[2,2,1,160,512]{4,3,1,0,2:T(8,128)(2,1)S(1)} %slice.235), channel_id=1, source_target_pairs={{16,0},{32,16},{48,32},{64,48},{80,64},{96,80},{112,96},{128,112},... | collective-permute-start | bytes 1966088 | tf_op jit(solution)/shard_map/ppermute | solution.py:12
  23.0 162.7 %collective-permute-start.2 = (bf16[2,5,1,160,512]{4,3,1,0,2:T(8,128)(2,1)}, bf16[2,5,1,160,512]{4,3,1,0,2:T(8,128)(2,1)}, u32[]{:S(2)}, u32[]{:S(2)}) collective-permute-start(bf16[2,5,1,160,512]{4,3,1,0,2:T(8,128)(2,1)} %pad_maximum_fusion), channel_id=1, source_target_pairs={{1,0},{2,1},{3,2},{4,3},{5,4},{6,5},{7,6},{8,7},{9,8},{10,9},{11,1... | collective-permute-start | bytes 4915208 | tf_op jit(solution)/shard_map/ppermute | solution.py:23
  24.3 161.4 %collective-permute-start.1 = (bf16[2,5,1,160,512]{4,3,1,0,2:T(8,128)(2,1)}, bf16[2,5,1,160,512]{4,3,1,0,2:T(8,128)(2,1)}, u32[]{:S(2)}, u32[]{:S(2)}) collective-permute-start(bf16[2,5,1,160,512]{4,3,1,0,2:T(8,128)(2,1)} %pad_maximum_fusion), channel_id=1, source_target_pairs={{0,1},{1,2},{2,3},{3,4},{4,5},{5,6},{6,7},{7,8},{8,9},{9,10},{10,1... | collective-permute-start | bytes 4915208 | tf_op jit(solution)/shard_map/ppermute | solution.py:20
  192.5 17.7 %copy-start.2 = (bf16[512,27,512]{2,0,1:T(8,128)(2,1)S(1)}, bf16[512,27,512]{2,0,1:T(8,128)(2,1)}, u32[]{:S(2)}) copy-start(bf16[512,27,512]{2,0,1:T(8,128)(2,1)} %all-gather.2.cloned.1.call-done) | copy-start | bytes 42467332
  196.0 17.4 %slice-start = ((s8[5160960]{0:T(1024)(128)(4,1)}), s8[4194304]{0:T(1024)(128)(4,1)S(1)}, s32[]{:S(2)}) async-start(s8[5160960]{0:T(1024)(128)(4,1)} %bitcast.288), calls=%async_computation.1 | async-start | bytes 8388608
  203.4 10.0 %slice-start.1 = ((s8[5160960]{0:T(1024)(128)(4,1)}), s8[966656]{0:T(1024)(128)(4,1)S(1)}, s32[]{:S(2)}) async-start(s8[5160960]{0:T(1024)(128)(4,1)} %bitcast.288), calls=%async_computation.2 | async-start | bytes 1933312
  251.7 2.0 copy-start.3
  251.7 2.0 copy-start.4
Sparse Core Ops, SparseCore 0:
  9.8 141.8 all-gather.1
